TPU v7x, 32 devices: a whole 2x2x4 slice. The times are simulated.
32 devices in a mesh: ctx: 8 (over z, y), fsdp: 4 (over x, core).
Axes of the slice: x: 2, y: 2, z: 4, core: 2. Of those that a mesh axis runs over, the one named last changes fastest.
Arguments:
- inputs: bfloat16 [16, 1024, 640], P('fsdp', 'ctx'), may hold values from -6 to 6
- cotangent: bfloat16 [16, 1024, 640], P('fsdp', 'ctx'), may hold values from -6 to 6
- lengths: int32 [16], P('fsdp'), may hold values from 256 to 1024, as said below
- query_weight: bfloat16 [640, 1024], P('fsdp'), may hold values from -0.25 to 0.25
- key_weight: bfloat16 [640, 256], P('fsdp'), may hold values from -0.25 to 0.25
- value_weight: bfloat16 [640, 256], P('fsdp'), may hold values from -0.25 to 0.25
- out_weight: bfloat16 [1024, 640], P('fsdp'), may hold values from -0.1875 to 0.1875
- gate_weight: bfloat16 [640, 2048], P('fsdp'), may hold values from -0.25 to 0.25
- up_weight: bfloat16 [640, 2048], P('fsdp'), may hold values from -0.25 to 0.25
- down_weight: bfloat16 [2048, 640], P('fsdp'), may hold values from -0.125 to 0.125
- pre_attn_gain: bfloat16 [640], P('fsdp'), may hold values from -0.5 to 0.5
- post_attn_gain: bfloat16 [640], P('fsdp'), may hold values from -0.5 to 0.5
- pre_ffw_gain: bfloat16 [640], P('fsdp'), may hold values from -0.5 to 0.5
- post_ffw_gain: bfloat16 [640], P('fsdp'), may hold values from -0.5 to 0.5
- query_gain: bfloat16 [256], P('fsdp'), may hold values from 0 to 0.796875
- key_gain: bfloat16 [256], P('fsdp'), may hold values from 0 to 0.796875
Outputs:
- outputs: bfloat16 [16, 1024, 640], P('fsdp', 'ctx')
- input_grad: bfloat16 [16, 1024, 640], P('fsdp', 'ctx')
- query_weight_grad: float32 [640, 1024], P('fsdp')
- key_weight_grad: float32 [640, 256], P('fsdp')
- value_weight_grad: float32 [640, 256], P('fsdp')
- out_weight_grad: float32 [1024, 640], P('fsdp')
- gate_weight_grad: float32 [640, 2048], P('fsdp')
- up_weight_grad: float32 [640, 2048], P('fsdp')
- down_weight_grad: float32 [2048, 640], P('fsdp')
- pre_attn_gain_grad: float32 [640], P('fsdp')
- post_attn_gain_grad: float32 [640], P('fsdp')
- pre_ffw_gain_grad: float32 [640], P('fsdp')
- post_ffw_gain_grad: float32 [640], P('fsdp')
- query_gain_grad: float32 [256], P('fsdp')
- key_gain_grad: float32 [256], P('fsdp')
Inputs may be any that keep to these rules, and one draw needn't show every extreme that they name: Sequence s has its first lengths[s] positions live; later keys are excluded from every softmax. In each aligned block of 4 sequences exactly one, drawn from the seed, has all 1024 positions live.
All inputs are finite; a program needn't handle non-finite values.
Results may differ from a plain program's by a relative error of at most 0.022.
Values may be sent and summed in bfloat16 or wider, within the bound.
A program may use at most 256 MiB of HBM per device.

v0:
```python
import math

import jax
import jax.numpy as jnp
from jax import lax
from jax.sharding import PartitionSpec as P

EPSILON = 1e-06
MASKED_SCORE = -1e30
ROPE_BASE = 1000000.0


def norm_gain(values, gain_vec):
    return (
        values
        * lax.rsqrt(jnp.mean(values * values, axis=-1, keepdims=True) + EPSILON)
        * (1.0 + gain_vec)
    )


def rotate(values, positions):
    half_dim = values.shape[-1] // 2
    inverse = ROPE_BASE ** (-(jnp.arange(half_dim).astype(jnp.float32) * 2.0) / values.shape[-1])
    angles = positions.astype(jnp.float32)[:, None] * inverse[None, :]
    cosine = jnp.cos(angles)[:, None, :]
    sine_part = jnp.sin(angles)[:, None, :]
    first_half = values[..., :half_dim]
    second_half = values[..., half_dim:]
    return jnp.concatenate(
        [
            first_half * cosine - second_half * sine_part,
            second_half * cosine + first_half * sine_part,
        ],
        axis=-1,
    )


def gelu_mix(gate_in, up_in):
    return jax.nn.gelu(gate_in, approximate=True) * up_in


def body(
    inputs,
    cotangent,
    lengths,
    query_weight,
    key_weight,
    value_weight,
    out_weight,
    gate_weight,
    up_weight,
    down_weight,
    pre_attn_gain,
    post_attn_gain,
    pre_ffw_gain,
    post_ffw_gain,
    query_gain,
    key_gain,
):
    seq_count, row_count, model_width = inputs.shape
    gathered = (
        lax.all_gather(query_weight, "fsdp", axis=0, tiled=True),
        lax.all_gather(key_weight, "fsdp", axis=0, tiled=True),
        lax.all_gather(value_weight, "fsdp", axis=0, tiled=True),
        lax.all_gather(out_weight, "fsdp", axis=0, tiled=True),
        lax.all_gather(gate_weight, "fsdp", axis=0, tiled=True),
        lax.all_gather(up_weight, "fsdp", axis=0, tiled=True),
        lax.all_gather(down_weight, "fsdp", axis=0, tiled=True),
        lax.all_gather(pre_attn_gain, "fsdp", axis=0, tiled=True),
        lax.all_gather(post_attn_gain, "fsdp", axis=0, tiled=True),
        lax.all_gather(pre_ffw_gain, "fsdp", axis=0, tiled=True),
        lax.all_gather(post_ffw_gain, "fsdp", axis=0, tiled=True),
        lax.all_gather(query_gain, "fsdp", axis=0, tiled=True),
        lax.all_gather(key_gain, "fsdp", axis=0, tiled=True),
    )
    (
        query_full,
        key_full,
        value_full,
        out_full,
        gate_full,
        up_full,
        down_full,
        gain_attn_in,
        gain_attn_out,
        gain_ffw_in,
        gain_ffw_out,
        gain_query,
        gain_key,
    ) = gathered
    gain_attn_in = gain_attn_in.astype(jnp.float32)
    gain_attn_out = gain_attn_out.astype(jnp.float32)
    gain_ffw_in = gain_ffw_in.astype(jnp.float32)
    gain_ffw_out = gain_ffw_out.astype(jnp.float32)
    gain_query = gain_query.astype(jnp.float32)
    gain_key = gain_key.astype(jnp.float32)
    head_dim = key_full.shape[1]
    head_count = query_full.shape[1] // head_dim
    seq_len = row_count * lax.axis_size("ctx")
    key_span = math.gcd(512, seq_len)
    att_scale = head_dim ** (-0.5)
    flat_rows = seq_count * row_count
    positions = lax.axis_index("ctx") * row_count + jnp.arange(row_count, dtype=jnp.int32)
    x_flat = inputs.astype(jnp.float32).reshape(flat_rows, model_width)
    attn_in, attn_in_back = jax.vjp(norm_gain, x_flat, gain_attn_in)
    attn_in_b = attn_in.astype(jnp.bfloat16)
    query_lin = jnp.dot(attn_in_b, query_full, preferred_element_type=jnp.float32)
    key_lin = jnp.dot(attn_in_b, key_full, preferred_element_type=jnp.float32)
    value_lin = jnp.dot(attn_in_b, value_full, preferred_element_type=jnp.float32)

    def query_side(lin_values, gain_vec):
        return rotate(
            norm_gain(lin_values.reshape(seq_count, row_count, head_count, head_dim), gain_vec),
            positions,
        )

    def key_side(lin_values, gain_vec):
        return rotate(
            norm_gain(lin_values.reshape(seq_count, row_count, 1, head_dim), gain_vec), positions
        )[:, :, 0, :]

    query_rot, query_side_back = jax.vjp(query_side, query_lin, gain_query)
    key_rot, key_side_back = jax.vjp(key_side, key_lin, gain_key)
    query_b = query_rot.astype(jnp.bfloat16)
    key_b = key_rot.astype(jnp.bfloat16)
    value_b = value_lin.reshape(seq_count, row_count, head_dim).astype(jnp.bfloat16)

    def allowed(key_begin, key_count):
        key_pos = key_begin + jnp.arange(key_count, dtype=jnp.int32)
        causal = key_pos[None, :] <= positions[:, None]
        live = key_pos[None, :] < lengths[:, None]
        return (causal[None] & live[:, None, :])[:, None]

    def raw_scores(key_piece):
        return (
            jnp.einsum("sqhd,skd->shqk", query_b, key_piece, preferred_element_type=jnp.float32)
            * att_scale
        )

    stat_shape = (seq_count, head_count, row_count)
    running_max = jnp.full(stat_shape, MASKED_SCORE, jnp.float32)
    key_piece = lax.all_gather(key_b, "ctx", axis=1, tiled=True)
    value_piece = lax.all_gather(value_b, "ctx", axis=1, tiled=True)
    mask_now = allowed(jnp.int32(0), key_piece.shape[1])
    scores = jnp.where(mask_now, raw_scores(key_piece), MASKED_SCORE)
    new_max = jnp.maximum(running_max, jnp.max(scores, axis=-1))
    weights = jnp.where(mask_now, jnp.exp(scores - new_max[..., None]), 0.0)
    new_sum = jnp.sum(weights, axis=-1)
    new_acc = jnp.einsum(
        "shqk,skd->shqd",
        weights.astype(jnp.bfloat16),
        value_piece,
        preferred_element_type=jnp.float32,
    )
    final_state = (new_max, new_sum, new_acc)
    final_max, final_sum, final_acc = final_state
    attended = final_acc / final_sum[..., None]
    log_total = final_max + jnp.log(final_sum)
    attended_b = (
        attended.transpose(0, 2, 1, 3)
        .reshape(flat_rows, head_count * head_dim)
        .astype(jnp.bfloat16)
    )
    attn_lin = jnp.dot(attended_b, out_full, preferred_element_type=jnp.float32)
    attn_post, attn_post_back = jax.vjp(norm_gain, attn_lin, gain_attn_out)
    middle = x_flat + attn_post
    ffw_in, ffw_in_back = jax.vjp(norm_gain, middle, gain_ffw_in)
    ffw_in_b = ffw_in.astype(jnp.bfloat16)
    gate_lin = jnp.dot(ffw_in_b, gate_full, preferred_element_type=jnp.float32)
    up_lin = jnp.dot(ffw_in_b, up_full, preferred_element_type=jnp.float32)
    hidden, hidden_back = jax.vjp(gelu_mix, gate_lin, up_lin)
    hidden_b = hidden.astype(jnp.bfloat16)
    ffw_out = jnp.dot(hidden_b, down_full, preferred_element_type=jnp.float32)
    ffw_post, ffw_post_back = jax.vjp(norm_gain, ffw_out, gain_ffw_out)
    outputs = (middle + ffw_post).astype(jnp.bfloat16).reshape(seq_count, row_count, model_width)
    grad_top = cotangent.astype(jnp.float32).reshape(flat_rows, model_width)
    d_ffw_out, grad_ffw_out_gain = ffw_post_back(grad_top)
    d_ffw_out_b = d_ffw_out.astype(jnp.bfloat16)
    grad_down = jnp.einsum("rf,rd->fd", hidden_b, d_ffw_out_b, preferred_element_type=jnp.float32)
    d_hidden = jnp.einsum("rd,fd->rf", d_ffw_out_b, down_full, preferred_element_type=jnp.float32)
    d_gate, d_up = hidden_back(d_hidden)
    d_gate_b = d_gate.astype(jnp.bfloat16)
    d_up_b = d_up.astype(jnp.bfloat16)
    grad_gate = jnp.einsum("rd,rf->df", ffw_in_b, d_gate_b, preferred_element_type=jnp.float32)
    grad_up = jnp.einsum("rd,rf->df", ffw_in_b, d_up_b, preferred_element_type=jnp.float32)
    d_ffw_in = jnp.einsum(
        "rf,df->rd", d_gate_b, gate_full, preferred_element_type=jnp.float32
    ) + jnp.einsum("rf,df->rd", d_up_b, up_full, preferred_element_type=jnp.float32)
    d_middle_part, grad_ffw_in_gain = ffw_in_back(d_ffw_in)
    d_middle = grad_top + d_middle_part
    d_attn_lin, grad_attn_out_gain = attn_post_back(d_middle)
    d_attn_b = d_attn_lin.astype(jnp.bfloat16)
    grad_projection = jnp.einsum(
        "ro,rd->od", attended_b, d_attn_b, preferred_element_type=jnp.float32
    )
    d_attended_b = (
        jnp.einsum("rd,od->ro", d_attn_b, out_full, preferred_element_type=jnp.float32)
        .astype(jnp.bfloat16)
        .reshape(seq_count, row_count, head_count, head_dim)
    )
    d_attended = d_attended_b.astype(jnp.float32)
    row_delta = jnp.einsum("sqhd,shqd->shq", d_attended, attended, precision=lax.Precision.HIGHEST)

    def key_grads(key_piece, value_piece, key_begin):
        mask_now = allowed(key_begin, key_piece.shape[1])
        probabilities = jnp.where(
            mask_now, jnp.exp(raw_scores(key_piece) - log_total[..., None]), 0.0
        )
        d_probs = jnp.einsum(
            "sqhd,skd->shqk", d_attended_b, value_piece, preferred_element_type=jnp.float32
        )
        d_scores = (probabilities * (d_probs - row_delta[..., None])).astype(jnp.bfloat16)
        d_query = (
            jnp.einsum("shqk,skd->sqhd", d_scores, key_piece, preferred_element_type=jnp.float32)
            * att_scale
        )
        d_key = (
            jnp.einsum("shqk,sqhd->skd", d_scores, query_b, preferred_element_type=jnp.float32)
            * att_scale
        )
        d_value = jnp.einsum(
            "shqk,sqhd->skd",
            probabilities.astype(jnp.bfloat16),
            d_attended_b,
            preferred_element_type=jnp.float32,
        )
        return (d_query, jnp.concatenate([d_key, d_value], axis=-1))

    key_back_all, value_back_all = (
        lax.all_gather(key_b, "ctx", axis=1, tiled=True),
        lax.all_gather(value_b, "ctx", axis=1, tiled=True),
    )

    def slice_keys(key_begin, key_count):
        return (
            lax.dynamic_slice_in_dim(key_back_all, key_begin, key_count, 1),
            lax.dynamic_slice_in_dim(value_back_all, key_begin, key_count, 1),
        )

    query_zero = jnp.zeros((seq_count, row_count, head_count, head_dim), jnp.float32)

    def joint_step(block_id, state):
        d_query_sum, key_buffer = state
        key_begin = block_id * key_span
        key_piece, value_piece = slice_keys(key_begin, key_span)
        d_query, d_keyval = key_grads(key_piece, value_piece, key_begin)
        return (
            d_query_sum + d_query,
            lax.dynamic_update_slice_in_dim(key_buffer, d_keyval, key_begin, 1),
        )

    d_query_rot, key_buffer = lax.fori_loop(
        0,
        seq_len // key_span,
        joint_step,
        (query_zero, jnp.zeros((seq_count, seq_len, 2 * head_dim), jnp.float32)),
    )
    d_keyval_own = lax.psum_scatter(key_buffer, "ctx", scatter_dimension=1, tiled=True)
    d_key_rot = d_keyval_own[..., :head_dim]
    d_value = d_keyval_own[..., head_dim:]
    d_query_lin, grad_query_gain = query_side_back(d_query_rot)
    d_key_lin, grad_key_gain = key_side_back(d_key_rot)
    d_query_b = d_query_lin.astype(jnp.bfloat16)
    d_key_b = d_key_lin.astype(jnp.bfloat16)
    d_value_b = d_value.reshape(flat_rows, head_dim).astype(jnp.bfloat16)
    grad_query = jnp.einsum("rd,rq->dq", attn_in_b, d_query_b, preferred_element_type=jnp.float32)
    grad_key = jnp.einsum("rd,rq->dq", attn_in_b, d_key_b, preferred_element_type=jnp.float32)
    grad_value = jnp.einsum("rd,rq->dq", attn_in_b, d_value_b, preferred_element_type=jnp.float32)
    d_attn_in = jnp.einsum("rq,dq->rd", d_query_b, query_full, preferred_element_type=jnp.float32)
    d_attn_in = d_attn_in + jnp.einsum(
        "rq,dq->rd", d_key_b, key_full, preferred_element_type=jnp.float32
    )
    d_attn_in = d_attn_in + jnp.einsum(
        "rq,dq->rd", d_value_b, value_full, preferred_element_type=jnp.float32
    )
    d_input_part, grad_attn_in_gain = attn_in_back(d_attn_in)
    input_grad = (
        (d_middle + d_input_part).astype(jnp.bfloat16).reshape(seq_count, row_count, model_width)
    )
    shards = (
        lax.psum_scatter(
            grad_query.astype(jnp.bfloat16), "fsdp", scatter_dimension=0, tiled=True
        ).astype(jnp.float32),
        lax.psum_scatter(
            grad_key.astype(jnp.bfloat16), "fsdp", scatter_dimension=0, tiled=True
        ).astype(jnp.float32),
        lax.psum_scatter(
            grad_value.astype(jnp.bfloat16), "fsdp", scatter_dimension=0, tiled=True
        ).astype(jnp.float32),
        lax.psum_scatter(
            grad_projection.astype(jnp.bfloat16), "fsdp", scatter_dimension=0, tiled=True
        ).astype(jnp.float32),
        lax.psum_scatter(
            grad_gate.astype(jnp.bfloat16), "fsdp", scatter_dimension=0, tiled=True
        ).astype(jnp.float32),
        lax.psum_scatter(
            grad_up.astype(jnp.bfloat16), "fsdp", scatter_dimension=0, tiled=True
        ).astype(jnp.float32),
        lax.psum_scatter(
            grad_down.astype(jnp.bfloat16), "fsdp", scatter_dimension=0, tiled=True
        ).astype(jnp.float32),
        lax.psum_scatter(
            grad_attn_in_gain.astype(jnp.bfloat16), "fsdp", scatter_dimension=0, tiled=True
        ).astype(jnp.float32),
        lax.psum_scatter(
            grad_attn_out_gain.astype(jnp.bfloat16), "fsdp", scatter_dimension=0, tiled=True
        ).astype(jnp.float32),
        lax.psum_scatter(
            grad_ffw_in_gain.astype(jnp.bfloat16), "fsdp", scatter_dimension=0, tiled=True
        ).astype(jnp.float32),
        lax.psum_scatter(
            grad_ffw_out_gain.astype(jnp.bfloat16), "fsdp", scatter_dimension=0, tiled=True
        ).astype(jnp.float32),
        lax.psum_scatter(
            grad_query_gain.astype(jnp.bfloat16), "fsdp", scatter_dimension=0, tiled=True
        ).astype(jnp.float32),
        lax.psum_scatter(
            grad_key_gain.astype(jnp.bfloat16), "fsdp", scatter_dimension=0, tiled=True
        ).astype(jnp.float32),
    )
    totals = lax.psum(
        (
            shards[0],
            shards[1],
            shards[2],
            shards[3],
            shards[4],
            shards[5],
            shards[6],
            shards[7],
            shards[8],
            shards[9],
            shards[10],
            shards[11],
            shards[12],
        ),
        "ctx",
    )
    return (outputs, input_grad) + tuple(totals)


def solution(mesh):
    in_specs = (
        P("fsdp", "ctx", None),
        P("fsdp", "ctx", None),
        P("fsdp"),
        P("fsdp", None),
        P("fsdp", None),
        P("fsdp", None),
        P("fsdp", None),
        P("fsdp", None),
        P("fsdp", None),
        P("fsdp", None),
        P("fsdp"),
        P("fsdp"),
        P("fsdp"),
        P("fsdp"),
        P("fsdp"),
        P("fsdp"),
    )
    out_specs = (
        P("fsdp", "ctx", None),
        P("fsdp", "ctx", None),
        P("fsdp", None),
        P("fsdp", None),
        P("fsdp", None),
        P("fsdp", None),
        P("fsdp", None),
        P("fsdp", None),
        P("fsdp", None),
        P("fsdp"),
        P("fsdp"),
        P("fsdp"),
        P("fsdp"),
        P("fsdp"),
        P("fsdp"),
    )
    return jax.shard_map(body, mesh=mesh, in_specs=in_specs, out_specs=out_specs, check_vma=False)
```

profile of v0, /device:TPU:0, one launch (start us, length us, event | category | flops | bytes accessed | tf_op | source)
XLA Modules:
  0.0 893.9 jit_solution(16385621297810421104)
XLA Ops:
  17.0 9.2 %all-reduce.18 = (bf16[256]{0:T(256)(128)(2,1)S(1)}, bf16[640]{0:T(1024)(128)(2,1)S(1)}, bf16[256]{0:T(256)(128)(2,1)S(1)}, bf16[640]{0:T(1024)(128)(2,1)S(1)}, ...) all-reduce(bf16[256]{0:T(256)(128)(2,1)S(1)} %dynamic-update-slice., ...), channel_id=1, replica_groups=mesh['ctx'=8,'fsdp'=4] {'fsdp'}, use_global_device_ids=true, to_apply=%add.5 | all-reduce | flops 3072 | bytes 12288
  26.3 6.2 all_gather.48
  36.3 6.2 all_gather.53
  58.8 27.3 %all-gather.21.cloned.1.call-done = bf16[4,1024,1,256]{3,1,0,2:T(8,128)(2,1)} async-done(((bf16[4,128,1,256]{3,1,0,2:T(8,128)(2,1)}), bf16[4,1024,1,256]{3,1,0,2:T(8,128)(2,1)}) %all-gather.21.cloned.1.call-update) | async-done | bytes 2097168 | tf_op jit(solution)/shard_map/all_gather | solution.py:142
  95.2 41.4 %all-gather.11.cloned.1.call-done = bf16[4,1024,256]{2,1,0:T(8,128)(2,1)} async-done(((bf16[4,128,256]{2,1,0:T(8,128)(2,1)}), bf16[4,1024,256]{2,1,0:T(8,128)(2,1)}) %all-gather.11.cloned.1.call-update) | async-done | bytes 2097168 | tf_op jit(solution)/shard_map/all_gather | solution.py:143
  136.6 8.1 fusion.45
  146.8 8.0 all-gather.13.cloned.1.call-done
  160.6 21.1 %all-gather.15.cloned.1.call-done = bf16[640,2048]{1,0:T(8,128)(2,1)} async-done(((bf16[160,2048]{1,0:T(8,128)(2,1)}), bf16[640,2048]{1,0:T(8,128)(2,1)}) %all-gather.15.cloned.1.call-update) | async-done | bytes 2621456 | tf_op jit(solution)/shard_map/all_gather | solution.py:66
  181.7 5.8 fusion.78
  187.5 21.2 %all-gather.17.cloned.1.call-done = bf16[640,2048]{1,0:T(8,128)(2,1)} async-done(((bf16[160,2048]{1,0:T(8,128)(2,1)}), bf16[640,2048]{1,0:T(8,128)(2,1)}) %all-gather.17.cloned.1.call-update) | async-done | bytes 2621456 | tf_op jit(solution)/shard_map/all_gather | solution.py:67
  208.7 8.3 multiply_convert_fusion.1
  217.0 18.9 %all-gather.19.cloned.1.call-done = bf16[2048,640]{1,0:T(8,128)(2,1)} async-done(((bf16[512,640]{1,0:T(8,128)(2,1)}), bf16[2048,640]{1,0:T(8,128)(2,1)}) %all-gather.19.cloned.1.call-update) | async-done | bytes 2621456 | tf_op jit(solution)/shard_map/all_gather | solution.py:68
  277.6 40.1 %while.16 = (s32[]{:T(128)}, f32[4,128,4,256]{1,3,2,0:T(8,128)S(1)}, f32[4,1024,512]{2,1,0:T(8,128)}, bf16[4,1024,256]{2,1,0:T(8,128)(2,1)}, s32[4]{0:T(128)S(1)...) while((s32[]{:T(128)}, ...), condition=%wide.region_12.13_spmd.clone, body=%wide.region_11.12_spmd.clone.sunk | while | flops 2698316288 | bytes 81694016 | solution.py:252
  287.9 5.3 copy.128
  307.8 5.3 copy.128
  338.2 4.9 convolution_convert_fusion
  348.6 5.6 reduce-scatter.11.cloned.1.call-done
  354.2 37.0 %reduce-scatter.19.cloned.1.call-done = bf16[160,2048]{1,0:T(8,128)(2,1)} async-done(((bf16[640,2048]{1,0:T(8,128)(2,1)}), bf16[160,2048]{1,0:T(8,128)(2,1)}) %reduce-scatter.19.cloned.1.call-update) | async-done | bytes 655376 | tf_op jit(solution)/shard_map/reduce_scatter | solution.py:293
  391.2 37.4 %reduce-scatter.21.cloned.1.call-done = bf16[160,2048]{1,0:T(8,128)(2,1)} async-done(((bf16[640,2048]{1,0:T(8,128)(2,1)}), bf16[160,2048]{1,0:T(8,128)(2,1)}) %reduce-scatter.21.cloned.1.call-update) | async-done | bytes 655376 | tf_op jit(solution)/shard_map/reduce_scatter | solution.py:296
  428.7 37.1 %reduce-scatter.23.cloned.1.call-done = bf16[512,640]{1,0:T(8,128)(2,1)} async-done(((bf16[2048,640]{1,0:T(8,128)(2,1)}), bf16[512,640]{1,0:T(8,128)(2,1)}) %reduce-scatter.23.cloned.1.call-update) | async-done | bytes 655376 | tf_op jit(solution)/shard_map/reduce_scatter | solution.py:299
  465.8 153.5 %reduce-scatter.9.cloned.1.call-done = f32[4,128,512]{2,1,0:T(8,128)} async-done(((f32[4,1024,512]{2,1,0:T(8,128)}), f32[4,128,512]{2,1,0:T(8,128)}) %reduce-scatter.9.cloned.1.call-update) | async-done | bytes 1048592 | tf_op jit(solution)/shard_map/reduce_scatter | solution.py:258
  627.0 7.1 all-reduce.17
  641.7 23.5 %reduce-scatter.13.cloned.1.call-done = bf16[160,256]{1,0:T(8,128)(2,1)} async-done(((bf16[640,256]{1,0:T(8,128)(2,1)}), bf16[160,256]{1,0:T(8,128)(2,1)}) %reduce-scatter.13.cloned.1.call-update) | async-done | bytes 81936 | tf_op jit(solution)/shard_map/reduce_scatter | solution.py:284
  665.2 221.7 %all-reduce.20 = (f32[160,1024]{1,0:T(8,128)}, f32[160,256]{1,0:T(8,128)}, f32[160,256]{1,0:T(8,128)}, f32[256,640]{1,0:T(8,128)}, f32[160,2048]{1,0:T(8,128)}, ...) all-reduce(bf16[160,1024]{1,0:T(8,128)(2,1)} %reduce-scatter.11.clo, ...), channel_id=1, replica_groups=mesh['ctx'=8,'fsdp'=4] {'ctx'}, use_global_device_ids=true, to_apply=%region_18.19 | all-reduce | flops 1393408 | bytes 8361984 | tf_op jit(solution)/shard_map/psum | solution.py:321
  (302 shorter events, 155.3 us)
Async XLA Ops:
  7.2 41.3 %all-gather.9.cloned.1.call-start = ((), (), s32[]{:S(2)}) async-start(), calls=%async_computation.8 | async-start | bytes 1638400 | tf_op jit(solution)/shard_map/all_gather | solution.py:62
  7.9 78.1 %all-gather.21.cloned.1.call-start = ((), (), s32[]{:S(2)}) async-start(), calls=%async_computation.22 | async-start | bytes 2359296 | tf_op jit(solution)/shard_map/all_gather | solution.py:142
  11.9 30.6 %copy-start.51 = (f32[4,128]{1,0:T(4,128)}, f32[4,128]{1,0:T(4,128)S(1)}, u32[]{:S(2)}) copy-start(f32[4,128]{1,0:T(4,128)S(1)} %fusion.58) | copy-start | bytes 6148
  11.9 20.5 %copy-start.47 = (f32[512]{0:T(512)}, f32[512]{0:T(512)S(1)}, u32[]{:S(2)}) copy-start(f32[512]{0:T(512)S(1)} %bitcast_rsqrt_fusion.1) | copy-start | bytes 6148
  34.7 19.6 %copy-start.25 = (f32[128,128]{1,0:T(8,128)}, f32[128,128]{1,0:T(8,128)S(1)}, u32[]{:S(2)}) copy-start(f32[128,128]{1,0:T(8,128)S(1)} %get-tuple-element.348) | copy-start | bytes 196612
  34.7 19.6 %copy-start.27 = (f32[128,128]{1,0:T(8,128)}, f32[128,128]{1,0:T(8,128)S(1)}, u32[]{:S(2)}) copy-start(f32[128,128]{1,0:T(8,128)S(1)} %get-tuple-element.349) | copy-start | bytes 196612
  36.2 100.4 %all-gather.11.cloned.1.call-start = ((), (), s32[]{:S(2)}) async-start(), calls=%async_computation.9 | async-start | bytes 2359296 | tf_op jit(solution)/shard_map/all_gather | solution.py:143
  43.9 110.9 %all-gather.13.cloned.1.call-start = ((), (), s32[]{:S(2)}) async-start(), calls=%async_computation.10 | async-start | bytes 1638400 | tf_op jit(solution)/shard_map/all_gather | solution.py:65
  44.4 137.3 %all-gather.15.cloned.1.call-start = ((), (), s32[]{:S(2)}) async-start(), calls=%async_computation.11 | async-start | bytes 3276800 | tf_op jit(solution)/shard_map/all_gather | solution.py:66
  45.0 163.7 %all-gather.17.cloned.1.call-start = ((), (), s32[]{:S(2)}) async-start(), calls=%async_computation.12 | async-start | bytes 3276800 | tf_op jit(solution)/shard_map/all_gather | solution.py:67
  45.6 190.3 %all-gather.19.cloned.1.call-start = ((), (), s32[]{:S(2)}) async-start(), calls=%async_computation.13 | async-start | bytes 3276800 | tf_op jit(solution)/shard_map/all_gather | solution.py:68
  46.4 302.2 %reduce-scatter.17.cloned.1.call-start = ((), (), s32[]{:S(2)}) async-start(), calls=%async_computation.18 | async-start | bytes 1638400 | tf_op jit(solution)/shard_map/reduce_scatter | solution.py:290
  270.2 84.0 %reduce-scatter.11.cloned.1.call-start = ((), (), s32[]{:S(2)}) async-start(), calls=%async_computation.15 | async-start | bytes 1638400 | tf_op jit(solution)/shard_map/reduce_scatter | solution.py:281
  327.4 63.9 %reduce-scatter.19.cloned.1.call-start = ((), (), s32[]{:S(2)}) async-start(), calls=%async_computation.19 | async-start | bytes 3276800 | tf_op jit(solution)/shard_map/reduce_scatter | solution.py:293
  332.0 96.6 %reduce-scatter.21.cloned.1.call-start = ((), (), s32[]{:S(2)}) async-start(), calls=%async_computation.20 | async-start | bytes 3276800 | tf_op jit(solution)/shard_map/reduce_scatter | solution.py:296
  337.1 128.6 %reduce-scatter.23.cloned.1.call-start = ((), (), s32[]{:S(2)}) async-start(), calls=%async_computation.21 | async-start | bytes 3276800 | tf_op jit(solution)/shard_map/reduce_scatter | solution.py:299
  343.1 276.1 %reduce-scatter.9.cloned.1.call-start = ((), (), s32[]{:S(2)}) async-start(), calls=%async_computation.14 | async-start | bytes 9437184 | tf_op jit(solution)/shard_map/reduce_scatter | solution.py:258
  343.9 297.8 %reduce-scatter.15.cloned.1.call-start = ((), (), s32[]{:S(2)}) async-start(), calls=%async_computation.17 | async-start | bytes 409600 | tf_op jit(solution)/shard_map/reduce_scatter | solution.py:287
  348.6 273.3 %copy-start.9 = (f32[512,256]{1,0:T(8,128)S(1)}, f32[512,256]{1,0:T(8,128)}, u32[]{:S(2)}) copy-start(f32[512,256]{1,0:T(8,128)} %copy-done.8) | copy-start | bytes 1572868
  348.6 273.3 %copy-start.50 = (f32[4,128]{1,0:T(4,128)S(1)}, f32[4,128]{1,0:T(4,128)}, u32[]{:S(2)}) copy-start(f32[4,128]{1,0:T(4,128)} %copy-done.49) | copy-start | bytes 6148
  348.6 273.3 %copy-start.57 = (f32[256]{0:T(256)S(1)}, f32[256]{0:T(256)}, u32[]{:S(2)}) copy-start(f32[256]{0:T(256)} %copy-done.56) | copy-start | bytes 3076
  621.8 43.4 %reduce-scatter.13.cloned.1.call-start = ((), (), s32[]{:S(2)}) async-start(), calls=%async_computation.16 | async-start | bytes 409600 | tf_op jit(solution)/shard_map/reduce_scatter | solution.py:284
  635.5 29.7 %copy-start.36 = (bf16[160,2048]{1,0:T(8,128)(2,1)S(1)}, bf16[160,2048]{1,0:T(8,128)(2,1)}, u32[]{:S(2)}) copy-start(bf16[160,2048]{1,0:T(8,128)(2,1)} %reduce-scatter.19.cloned.1.call-done) | copy-start | bytes 1966084
  635.5 29.7 %copy-start.37 = (bf16[160,2048]{1,0:T(8,128)(2,1)S(1)}, bf16[160,2048]{1,0:T(8,128)(2,1)}, u32[]{:S(2)}) copy-start(bf16[160,2048]{1,0:T(8,128)(2,1)} %reduce-scatter.21.cloned.1.call-done) | copy-start | bytes 1966084
  (62 other events, 193.3 us)
Sparse Core Ops, SparseCore 0:
  9.6 21.7 all-gather.8
  36.3 49.7 all-gather.20
  88.8 47.7 all-gather.10
  138.0 16.6 all-gather.12
  156.1 25.5 all-gather.14
  183.1 25.5 all-gather.16
  210.3 25.5 all-gather.18
  270.3 26.5 reduce-scatter.16
  327.5 26.6 reduce-scatter.10
  356.6 34.6 reduce-scatter.18
  393.9 34.6 reduce-scatter.20
  431.1 34.6 reduce-scatter.22
  469.8 149.3 reduce-scatter.8
  622.2 19.4 reduce-scatter.14
  644.7 20.4 reduce-scatter.12
where the time goes:
time: 902 us; the launch traced here: 894 us
  waiting for transfers between devices  439 us (49%)
  blocking collectives  250 us (28%)
  matrix products  88.7 us (10%)
  local copies, waits for them, and re-layouts  62.2 us (7%)
  other arithmetic  34.2 us (4%)
  between operations  17.9 us (2%)
    psum x1, blocking collectives, body(): lax.psum((shards[0], shards[1], shards[2], shards[3], shards[4], shards[5...  222 us
    reduce_scatter x1, waiting for transfers between devices, body(): lax.psum_scatter(key_buffer, 'ctx', scatter_dimension=1, tiled=True)  154 us
    all_gather x1, waiting for transfers between devices, body(): value_piece = lax.all_gather(value_b, 'ctx', axis=1, tiled=True)  41.4 us
    reduce_scatter x1, waiting for transfers between devices, body(): lax.psum_scatter(grad_up.astype(jnp.bfloat16), 'fsdp', scatter_dimension=...  37.4 us
    reduce_scatter x1, waiting for transfers between devices, body(): lax.psum_scatter(grad_down.astype(jnp.bfloat16), 'fsdp', scatter_dimensio...  37.1 us
    reduce_scatter x1, waiting for transfers between devices, body(): lax.psum_scatter(grad_gate.astype(jnp.bfloat16), 'fsdp', scatter_dimensio...  37 us
    all_gather x1, waiting for transfers between devices, body(): key_piece = lax.all_gather(key_b, 'ctx', axis=1, tiled=True)  27.3 us
    unnamed x147, local copies, waits for them, and re-layouts  25.9 us
  transfers between devices with their start and end apart: 15, of which 13 were waited for; matrix products, arithmetic and copies ran while one was open for 15% of the time, Pallas kernels for 0%

commit v1 on v0

--- a/solution.py
+++ b/solution.py
@@ -3,6 +3,8 @@
 import jax
 import jax.numpy as jnp
 from jax import lax
+from jax.experimental import pallas as pl
+from jax.experimental.pallas import tpu as pltpu
 from jax.sharding import PartitionSpec as P
 
 EPSILON = 1e-06
@@ -33,6 +35,212 @@
         ],
         axis=-1,
     )
+
+
+MESH_ID = pl.DeviceIdType.MESH
+VMEM_BYTES = 56 * 1024 * 1024
+
+
+def place():
+    ctx = lax.axis_index("ctx")
+    fsdp = lax.axis_index("fsdp")
+    return lax.rem(ctx, 2), lax.div(ctx, 2), lax.rem(fsdp, 2), lax.div(fsdp, 2)
+
+
+def device(y, z, core, x):
+    return (z * 2 + y, x * 2 + core)
+
+
+def greet(peers):
+    barrier = pltpu.get_barrier_semaphore()
+    for peer in peers:
+        pl.semaphore_signal(barrier, inc=1, device_id=peer, device_id_type=MESH_ID)
+    pl.semaphore_wait(barrier, len(peers))
+
+
+def reduce_kernel(by_columns, *refs):
+    count = len(by_columns)
+    grads, gains = refs[:count], refs[count]
+    outs, gain_out = refs[count + 1 : 2 * count + 1], refs[2 * count + 1]
+    refs = refs[2 * count + 2 :]
+    core_in, x_in, y_in, z_in = (refs[i * count : (i + 1) * count] for i in range(4))
+    gain_in, gain_sum, send_sem, recv_sem, gain_send, gain_recv = refs[4 * count :]
+    y, z, core, x = place()
+    core_peer = device(y, z, 1 - core, x)
+    x_peer = device(y, z, core, 1 - x)
+    y_peer = device(1 - y, z, core, x)
+    z_at = [lax.rem(z + hop, 4) for hop in (1, 2, 3)]
+    z_peers = [device(y, other, core, x) for other in z_at]
+    greet([core_peer, x_peer, y_peer] + z_peers)
+
+    def quarter(item, ref, at):
+        if by_columns[item]:
+            width = ref.shape[1] // 4
+            return ref.at[:, pl.ds(pl.multiple_of(at * width, 128), width)]
+        width = ref.shape[0] // 4
+        return ref.at[pl.ds(pl.multiple_of(at * width, 16), width), :]
+
+    def copy(item, slot, source, target, peer):
+        return pltpu.make_async_remote_copy(
+            src_ref=source,
+            dst_ref=target,
+            send_sem=send_sem.at[item, slot],
+            recv_sem=recv_sem.at[item, slot],
+            device_id=peer,
+            device_id_type=MESH_ID,
+        )
+
+    def gain_copy(slot, source, peer):
+        return pltpu.make_async_remote_copy(
+            src_ref=source,
+            dst_ref=gain_in.at[slot],
+            send_sem=gain_send.at[slot],
+            recv_sem=gain_recv.at[slot],
+            device_id=peer,
+            device_id_type=MESH_ID,
+        )
+
+    def add_rows(target, others):
+        rows = target.shape[0]
+
+        @pl.loop(0, rows // 16)
+        def _(step):
+            span = pl.ds(pl.multiple_of(step * 16, 16), 16)
+            total = others[0][span, :].astype(jnp.float32)
+            for other in others[1:]:
+                total = total + other[span, :].astype(jnp.float32)
+            target[span, :] = total.astype(target.dtype)
+
+    copies = [[None] * 10 for _ in range(count)]
+    gain_copies = [None] * 6
+
+    def stage_core(item):
+        copies[item][0] = copy(item, 0, grads[item].at[:, 1 - core], core_in[item], core_peer)
+        copies[item][0].start()
+
+    def stage_x(item):
+        copies[item][0].wait_recv()
+        for side in range(2):
+            for half in range(2):
+                target = core_in[item].at[side, half]
+                add_rows(target, [target, grads[item].at[side, core, half]])
+        copies[item][1] = copy(item, 1, core_in[item].at[1 - x], x_in[item], x_peer)
+        copies[item][1].start()
+
+    def stage_y(item):
+        copies[item][1].wait_recv()
+        for half in range(2):
+            target = x_in[item].at[half]
+            add_rows(target, [target, core_in[item].at[x, half]])
+        copies[item][2] = copy(item, 2, x_in[item].at[1 - y], y_in[item], y_peer)
+        copies[item][2].start()
+
+    def stage_z(item):
+        copies[item][2].wait_recv()
+        add_rows(y_in[item], [y_in[item], x_in[item].at[y]])
+        for hop in range(3):
+            copies[item][3 + hop] = copy(
+                item, 3 + hop, quarter(item, y_in[item], z_at[hop]), z_in[item].at[hop], z_peers[hop]
+            )
+            copies[item][3 + hop].start()
+
+    def stage_back_z(item):
+        for hop in range(3):
+            copies[item][3 + hop].wait_recv()
+        mine = quarter(item, outs[item].at[y], z)
+        add_rows(mine, [quarter(item, y_in[item], z)] + [z_in[item].at[hop] for hop in range(3)])
+        for hop in range(3):
+            copies[item][6 + hop] = copy(item, 6 + hop, mine, mine, z_peers[hop])
+            copies[item][6 + hop].start()
+
+    def stage_back_y(item):
+        for hop in range(3):
+            copies[item][6 + hop].wait_recv()
+        copies[item][9] = copy(item, 9, outs[item].at[y], outs[item].at[y], y_peer)
+        copies[item][9].start()
+
+    def gain_step(step):
+        if step == 0:
+            gain_copies[0] = gain_copy(0, gains, core_peer)
+            gain_copies[0].start()
+        elif step <= 2:
+            gain_copies[step - 1].wait_recv()
+            before = gains if step == 1 else gain_sum.at[step - 2]
+            gain_sum[step - 1] = before[...] + gain_in[step - 1]
+            gain_copies[step] = gain_copy(step, gain_sum.at[step - 1], (x_peer, y_peer)[step - 1])
+            gain_copies[step].start()
+        elif step == 3:
+            gain_copies[2].wait_recv()
+            gain_sum[2] = gain_sum[1] + gain_in[2]
+            for hop in range(3):
+                gain_copies[3 + hop] = gain_copy(3 + hop, gain_sum.at[2], z_peers[hop])
+                gain_copies[3 + hop].start()
+        elif step == 4:
+            for hop in range(3):
+                gain_copies[3 + hop].wait_recv()
+            gain_out[...] = (gain_sum[2] + gain_in[4]) + (gain_in[3] + gain_in[5])
+
+    for item in range(count):
+        stage_core(item)
+    stages = (stage_x, stage_y, stage_z, stage_back_z, stage_back_y)
+    for tick in range(count + len(stages) - 1):
+        for at, stage in enumerate(stages):
+            if 0 <= tick - at < count:
+                stage(tick - at)
+        gain_step(tick)
+    for item in range(count):
+        copies[item][9].wait_recv()
+    for item in range(count):
+        for slot in range(10):
+            copies[item][slot].wait_send()
+    for slot in range(6):
+        gain_copies[slot].wait_send()
+
+
+def reduce_all(grads, by_columns, gains):
+    shaped, outs, scratch = [], [], [[], [], [], []]
+    for grad, columns_split in zip(grads, by_columns):
+        rows, columns = grad.shape[0] // 8, grad.shape[1]
+        shaped.append(grad.reshape(2, 2, 2, rows, columns))
+        outs.append(jax.ShapeDtypeStruct((2, rows, columns), jnp.bfloat16))
+        piece = (rows, columns // 4) if columns_split else (rows // 4, columns)
+        scratch[0].append(pltpu.VMEM((2, 2, rows, columns), jnp.bfloat16))
+        scratch[1].append(pltpu.VMEM((2, rows, columns), jnp.bfloat16))
+        scratch[2].append(pltpu.VMEM((rows, columns), jnp.bfloat16))
+        scratch[3].append(pltpu.VMEM((3,) + piece, jnp.bfloat16))
+    count = len(grads)
+    outs.append(jax.ShapeDtypeStruct(gains.shape, jnp.float32))
+    sent = sum(grad.size for grad in grads)
+
+    def kernel(*refs):
+        reduce_kernel(by_columns, *refs)
+
+    results = pl.pallas_call(
+        kernel,
+        out_shape=outs,
+        in_specs=[pl.BlockSpec(memory_space=pltpu.VMEM)] * (count + 1),
+        out_specs=[pl.BlockSpec(memory_space=pltpu.VMEM)] * (count + 1),
+        scratch_shapes=scratch[0]
+        + scratch[1]
+        + scratch[2]
+        + scratch[3]
+        + [
+            pltpu.VMEM((6,) + gains.shape, jnp.float32),
+            pltpu.VMEM((3,) + gains.shape, jnp.float32),
+            pltpu.SemaphoreType.DMA((count, 10)),
+            pltpu.SemaphoreType.DMA((count, 10)),
+            pltpu.SemaphoreType.DMA((6,)),
+            pltpu.SemaphoreType.DMA((6,)),
+        ],
+        compiler_params=pltpu.CompilerParams(
+            collective_id=1, has_side_effects=True, vmem_limit_bytes=VMEM_BYTES
+        ),
+        cost_estimate=pl.CostEstimate(flops=2 * sent, bytes_accessed=4 * sent, transcendentals=0),
+        name="reduce_grads",
+    )(*shaped, gains)
+    return [
+        result.reshape(2 * result.shape[1], result.shape[2]) for result in results[:-1]
+    ] + [results[-1]]
 
 
 def gelu_mix(gate_in, up_in):
@@ -58,6 +266,7 @@
     key_gain,
 ):
     seq_count, row_count, model_width = inputs.shape
+    fast = lax.axis_size("ctx") == 8 and lax.axis_size("fsdp") == 4
     gathered = (
         lax.all_gather(query_weight, "fsdp", axis=0, tiled=True),
         lax.all_gather(key_weight, "fsdp", axis=0, tiled=True),
@@ -277,6 +486,44 @@
     input_grad = (
         (d_middle + d_input_part).astype(jnp.bfloat16).reshape(seq_count, row_count, model_width)
     )
+    if fast:
+        gain_rows = [
+            grad_attn_in_gain,
+            grad_attn_out_gain,
+            grad_ffw_in_gain,
+            grad_ffw_out_gain,
+            jnp.pad(grad_query_gain, (0, model_width - head_dim)),
+            jnp.pad(grad_key_gain, (0, model_width - head_dim)),
+        ]
+        gain_pack = jnp.pad(jnp.stack(gain_rows), ((0, 2), (0, 0)))
+        grads_in = jnp.concatenate([grad_query, grad_key, grad_value], axis=1)
+        t_down, t_gate, t_up, t_projection, t_in, gain_totals = reduce_all(
+            [
+                grad_down.astype(jnp.bfloat16),
+                grad_gate.astype(jnp.bfloat16),
+                grad_up.astype(jnp.bfloat16),
+                grad_projection.astype(jnp.bfloat16),
+                grads_in.astype(jnp.bfloat16),
+            ],
+            (False, True, True, False, True),
+            gain_pack,
+        )
+        part = lax.axis_index("fsdp")
+        wide = head_count * head_dim
+        results = [
+            t_in[:, :wide],
+            t_in[:, wide : wide + head_dim],
+            t_in[:, wide + head_dim :],
+            t_projection,
+            t_gate,
+            t_up,
+            t_down,
+        ]
+        results = [item.astype(jnp.float32) for item in results]
+        for at in range(6):
+            size = (model_width if at < 4 else head_dim) // 4
+            results.append(lax.dynamic_slice_in_dim(gain_totals[at], part * size, size, 0))
+        return (outputs, input_grad) + tuple(results)
     shards = (
         lax.psum_scatter(
             grad_query.astype(jnp.bfloat16), "fsdp", scatter_dimension=0, tiled=True

time: 902 us -> 620 us (0.69)
  blocking collectives: 250 us -> 21.6 us
  waiting for transfers between devices: 439 us -> 273 us
  Pallas kernels: 0 us -> 121 us
    psum x1 -> x0, blocking collectives: 222 us -> none  [body(): lax.psum((shards[0], shards[1], shards[2], shards[3], shards[4], shards[5...]
    reduce_scatter x7 -> x0, waiting for transfers between devices: 144 us -> none  [the longest x1 37.4 us: body(): lax.psum_scatter(grad_up.astype(jnp.bfloat16), 'fsdp', scatter_dimension=...]
    pallas_call x0 -> x1, Pallas kernels: none -> 121 us  [reduce_all(): pl.pallas_call(kernel, out_shape=outs, in_specs=[pl.BlockSpec(memory_spac...]
    reduce_scatter x1, waiting for transfers between devices: 154 us -> 122 us  [body(): lax.psum_scatter(key_buffer, 'ctx', scatter_dimension=1, tiled=True)]
    unnamed x147 -> x185, local copies, waits for them, and re-layouts: 25.9 us -> 23 us
  transfers between devices with their start and end apart: 15 -> 8, of which waited for: 13 -> 7; matrix products, arithmetic and copies ran while one was open for 15% -> 12% of each run, Pallas kernels for 0% -> 0%
where the time goes in v1:
time: 620 us; the launch traced here: 616 us
  waiting for transfers between devices  273 us (44%)
  Pallas kernels  121 us (20%)
  matrix products  81.2 us (13%)
  local copies, waits for them, and re-layouts  64.7 us (10%)
  other arithmetic  36.7 us (6%)
  blocking collectives  21.6 us (3%)
  between operations  17 us (3%)
    reduce_scatter x1, waiting for transfers between devices, body(): lax.psum_scatter(key_buffer, 'ctx', scatter_dimension=1, tiled=True)  122 us
    pallas_call x1, Pallas kernels, reduce_all(): pl.pallas_call(kernel, out_shape=outs, in_specs=[pl.BlockSpec(memory_spac...  121 us
    all_gather x1, waiting for transfers between devices, body(): value_piece = lax.all_gather(value_b, 'ctx', axis=1, tiled=True)  42 us
    all_gather x1, waiting for transfers between devices, body(): key_piece = lax.all_gather(key_b, 'ctx', axis=1, tiled=True)  31.3 us
    all_gather x1, waiting for transfers between devices, body(): lax.all_gather(gate_weight, 'fsdp', axis=0, tiled=True)  23.3 us
    unnamed x185, local copies, waits for them, and re-layouts  23 us
    all_gather x1, waiting for transfers between devices, body(): lax.all_gather(up_weight, 'fsdp', axis=0, tiled=True)  21.5 us
    all_gather x1, waiting for transfers between devices, body(): lax.all_gather(down_weight, 'fsdp', axis=0, tiled=True)  20.5 us
  transfers between devices with their start and end apart: 8, of which 7 were waited for; matrix products, arithmetic and copies ran while one was open for 12% of the time, Pallas kernels for 0%

profile of v1, /device:TPU:0, one launch (start us, length us, event | category | flops | bytes accessed | tf_op | source)
XLA Modules:
  0.0 616.1 jit_solution(17295887101998292458)
XLA Ops:
  16.9 9.2 %all-reduce.13 = (bf16[256]{0:T(256)(128)(2,1)S(1)}, bf16[640]{0:T(1024)(128)(2,1)S(1)}, bf16[256]{0:T(256)(128)(2,1)S(1)}, bf16[640]{0:T(1024)(128)(2,1)S(1)}, ...) all-reduce(bf16[256]{0:T(256)(128)(2,1)S(1)} %dynamic-update-slice., ...), channel_id=1, replica_groups=mesh['ctx'=8,'fsdp'=4] {'fsdp'}, use_global_device_ids=true, to_apply=%add.8 | all-reduce | flops 3072 | bytes 12288
  26.1 6.2 %all_gather.48 = bf16[640,256]{1,0:T(8,128)(2,1)S(1)} all-gather(bf16[160,256]{1,0:T(8,128)(2,1)} %param.22), channel_id=1, replica_groups=mesh['ctx'=8,'fsdp'=4] {'fsdp'}, dimensions={0}, use_global_device_ids=true | all-gather | bytes 409600 | tf_op jit(solution)/shard_map/all_gather | solution.py:272
  36.2 6.2 %all_gather.53 = bf16[640,256]{1,0:T(8,128)(2,1)S(1)} all-gather(bf16[160,256]{1,0:T(8,128)(2,1)S(1)} %copy-done.52), channel_id=1, replica_groups=mesh['ctx'=8,'fsdp'=4] {'fsdp'}, dimensions={0}, use_global_device_ids=true | all-gather | bytes 409600 | tf_op jit(solution)/shard_map/all_gather | solution.py:273
  54.7 31.3 %all-gather.21.cloned.1.call-done = bf16[4,1024,1,256]{3,1,0,2:T(8,128)(2,1)} async-done(((bf16[4,128,1,256]{3,1,0,2:T(8,128)(2,1)}), bf16[4,1024,1,256]{3,1,0,2:T(8,128)(2,1)}) %all-gather.21.cloned.1.call-update) | async-done | bytes 2097168 | tf_op jit(solution)/shard_map/all_gather | solution.py:351
  94.6 42.0 %all-gather.11.cloned.1.call-done = bf16[4,1024,256]{2,1,0:T(8,128)(2,1)} async-done(((bf16[4,128,256]{2,1,0:T(8,128)(2,1)}), bf16[4,1024,256]{2,1,0:T(8,128)(2,1)}) %all-gather.11.cloned.1.call-update) | async-done | bytes 2097168 | tf_op jit(solution)/shard_map/all_gather | solution.py:352
  136.5 8.1 %fusion.45 = (bf16[4,128,4,256]{3,1,2,0:T(8,128)(2,1)S(1)}, f32[4,4,128,256]{3,2,1,0:T(8,128)}) fusion(f32[4,128,4]{1,2,0:T(4,128)S(1)} %bitcast.287, bf16[4,1024,256]{2,1,0:T(8,128)(2,1)} %all-gather.11.cloned.1.call-done, f32[4,1024,128,4]{2,1,3,0:T(8,128)} %copy-done.15, f32[4,4,128]{2,1,0:T(4,128)S(1)} %broadcast_maximum_fusion, ...), kind=kOutput, calls=%fused_computation.63 | convolution fusion | flops 1085276160 | bytes 14172160 | tf_op jit(solution)/shard_map/shqk,skd->shqd/dot_general | solution.py:358
  145.7 9.0 %all-gather.13.cloned.1.call-done = bf16[1024,640]{1,0:T(8,128)(2,1)} async-done(((bf16[256,640]{1,0:T(8,128)(2,1)}), bf16[1024,640]{1,0:T(8,128)(2,1)}) %all-gather.13.cloned.1.call-update) | async-done | bytes 1310736 | tf_op jit(solution)/shard_map/all_gather | solution.py:274
  158.3 23.3 %all-gather.15.cloned.1.call-done = bf16[640,2048]{1,0:T(8,128)(2,1)} async-done(((bf16[160,2048]{1,0:T(8,128)(2,1)}), bf16[640,2048]{1,0:T(8,128)(2,1)}) %all-gather.15.cloned.1.call-update) | async-done | bytes 2621456 | tf_op jit(solution)/shard_map/all_gather | solution.py:275
  181.7 5.5 fusion.81
  187.1 21.5 %all-gather.17.cloned.1.call-done = bf16[640,2048]{1,0:T(8,128)(2,1)} async-done(((bf16[160,2048]{1,0:T(8,128)(2,1)}), bf16[640,2048]{1,0:T(8,128)(2,1)}) %all-gather.17.cloned.1.call-update) | async-done | bytes 2621456 | tf_op jit(solution)/shard_map/all_gather | solution.py:276
  208.7 6.7 %multiply_convert_fusion.1 = (bf16[512,2048]{1,0:T(8,128)(2,1)}, f32[512,2048]{1,0:T(8,128)}) fusion(f32[512,2048]{1,0:T(8,128)} %fusion.81, bf16[512,640]{1,0:T(8,128)(2,1)S(1)} %multiply_convert_fusion.2, bf16[640,2048]{1,0:T(8,128)(2,1)} %all-gather.17.cloned.1.call-done), kind=kOutput, calls=%fused_computation.50 | convolution fusion | flops 1352663040 | bytes 13762560 | tf_op jit(solution)/shard_map/dot_general | solution.py:379
  215.3 20.5 %all-gather.19.cloned.1.call-done = bf16[2048,640]{1,0:T(8,128)(2,1)} async-done(((bf16[512,640]{1,0:T(8,128)(2,1)}), bf16[2048,640]{1,0:T(8,128)(2,1)}) %all-gather.19.cloned.1.call-update) | async-done | bytes 2621456 | tf_op jit(solution)/shard_map/all_gather | solution.py:277
  235.8 4.4 multiply_reduce_fusion.8
  243.3 4.6 multiply_convert_fusion
  263.0 4.5 broadcast_in_dim.140.clone
  267.5 46.9 %while.16 = (s32[]{:T(128)}, f32[4,128,4,256]{1,3,2,0:T(8,128)}, f32[4,1024,512]{2,1,0:T(8,128)}, bf16[4,1024,256]{2,1,0:T(8,128)(2,1)}, s32[4]{0:T(128)S(1)}, /...) while((s32[]{:T(128)}, f32[4,128,4,256]{1,3,2,0:T(8,128)}, ...), condition=%wide.region_12.13_spmd.clone, body=%wide.region_11.12_spmd.clone.sunk | while | flops 2698316288 | bytes 111054208 | solution.py:461
  273.0 3.5 bitcast_add_fusion.4
  280.7 5.2 copy.119
  286.0 4.6 constant_dynamic-update-slice_fusion.2
  296.0 4.1 bitcast_add_fusion.4
  304.4 5.2 copy.119
  309.7 4.7 constant_dynamic-update-slice_fusion.2
  341.7 122.3 %reduce-scatter.2.cloned.1.call-done = f32[4,128,512]{2,1,0:T(8,128)} async-done(((f32[4,1024,512]{2,1,0:T(8,128)}), f32[4,128,512]{2,1,0:T(8,128)}) %reduce-scatter.2.cloned.1.call-update) | async-done | bytes 1048592 | tf_op jit(solution)/shard_map/reduce_scatter | solution.py:467
  473.5 121.1 %reduce_grads.1 = (bf16[2,256,640]{2,1,0:T(8,128)(2,1)}, bf16[2,80,2048]{2,1,0:T(8,128)(2,1)}, bf16[2,80,2048]{2,1,0:T(8,128)(2,1)}, bf16[2,128,640]{2,1,0:T(8,1...) custom-call(bf16[2,2,2,256,640]{4,3,2,1,0:T(8,128)(2,1)} %bitcast.269, bf16[2,2,2,80,2048]{4,3,2,1,0:T(8,128)(2,1)} %bitcast.270, ...), custom_call_target="tpu_custom_call" | custom-call | flops 11141120 | bytes 22282240 | tf_op jit(solution)/shard_map/reduce_grads/pallas_call | solution.py:218
  (346 shorter events, 125.3 us)
Async XLA Ops:
  7.2 41.3 %all-gather.9.cloned.1.call-start = ((), (), s32[]{:S(2)}) async-start(), calls=%async_computation.1 | async-start | bytes 1638400 | tf_op jit(solution)/shard_map/all_gather | solution.py:271
  7.9 78.1 %all-gather.21.cloned.1.call-start = ((), (), s32[]{:S(2)}) async-start(), calls=%async_computation.8 | async-start | bytes 2359296 | tf_op jit(solution)/shard_map/all_gather | solution.py:351
  11.8 30.6 %copy-start.60 = (f32[4,128]{1,0:T(4,128)}, f32[4,128]{1,0:T(4,128)S(1)}, u32[]{:S(2)}) copy-start(f32[4,128]{1,0:T(4,128)S(1)} %fusion.58) | copy-start | bytes 6148
  26.1 9.1 %copy-start.71 = (f32[256]{0:T(256)}, f32[256]{0:T(256)S(1)}, u32[]{:S(2)}) copy-start(f32[256]{0:T(256)S(1)} %convert_add_fusion.6) | copy-start | bytes 3076
  26.1 9.1 %copy-start.56 = (f32[512]{0:T(512)}, f32[512]{0:T(512)S(1)}, u32[]{:S(2)}) copy-start(f32[512]{0:T(512)S(1)} %bitcast_rsqrt_fusion.1) | copy-start | bytes 6148
  32.3 10.1 %copy-start.50 = (f32[640]{0:T(1024)}, f32[640]{0:T(1024)S(1)}, u32[]{:S(2)}) copy-start(f32[640]{0:T(1024)S(1)} %convert_add_fusion.4) | copy-start | bytes 7684
  33.8 8.6 %copy-start.5 = (bf16[4,128,640]{2,1,0:T(8,128)(2,1)S(1)}, bf16[4,128,640]{2,1,0:T(8,128)(2,1)}, u32[]{:S(2)}) copy-start(bf16[4,128,640]{2,1,0:T(8,128)(2,1)} %param.18) | copy-start | bytes 1966084
  34.6 17.1 %copy-start.25 = (f32[128,128]{1,0:T(8,128)}, f32[128,128]{1,0:T(8,128)S(1)}, u32[]{:S(2)}) copy-start(f32[128,128]{1,0:T(8,128)S(1)} %get-tuple-element.338) | copy-start | bytes 196612
  36.1 100.4 %all-gather.11.cloned.1.call-start = ((), (), s32[]{:S(2)}) async-start(), calls=%async_computation.2 | async-start | bytes 2359296 | tf_op jit(solution)/shard_map/all_gather | solution.py:352
  42.7 7.5 %copy-start.7 = (bf16[4,128,640]{2,1,0:T(8,128)(2,1)}, bf16[4,128,640]{2,1,0:T(8,128)(2,1)S(1)}, u32[]{:S(2)}) copy-start(bf16[4,128,640]{2,1,0:T(8,128)(2,1)S(1)} %fusion.60) | copy-start | bytes 1966084
  43.8 110.9 %all-gather.13.cloned.1.call-start = ((), (), s32[]{:S(2)}) async-start(), calls=%async_computation.3 | async-start | bytes 1638400 | tf_op jit(solution)/shard_map/all_gather | solution.py:274
  44.4 137.3 %all-gather.15.cloned.1.call-start = ((), (), s32[]{:S(2)}) async-start(), calls=%async_computation.4 | async-start | bytes 3276800 | tf_op jit(solution)/shard_map/all_gather | solution.py:275
  44.9 163.7 %all-gather.17.cloned.1.call-start = ((), (), s32[]{:S(2)}) async-start(), calls=%async_computation.5 | async-start | bytes 3276800 | tf_op jit(solution)/shard_map/all_gather | solution.py:276
  45.5 190.3 %all-gather.19.cloned.1.call-start = ((), (), s32[]{:S(2)}) async-start(), calls=%async_computation.6 | async-start | bytes 3276800 | tf_op jit(solution)/shard_map/all_gather | solution.py:277
  46.3 417.7 %reduce-scatter.2.cloned.1.call-start = ((), (), s32[]{:S(2)}) async-start(), calls=%async_computation.7 | async-start | bytes 9437184 | tf_op jit(solution)/shard_map/reduce_scatter | solution.py:467
  145.7 11.4 %copy-start.34 = (bf16[64,8,4,256]{3,1,2,0:T(8,128)(2,1)}, bf16[64,8,4,256]{3,1,2,0:T(8,128)(2,1)S(1)}, u32[]{:S(2)}) copy-start(bf16[64,8,4,256]{3,1,2,0:T(8,128)(2,1)S(1)} %copy.115) | copy-start | bytes 3145732
  158.3 50.4 %copy-start.41 = (bf16[512,640]{1,0:T(8,128)(2,1)}, bf16[512,640]{1,0:T(8,128)(2,1)S(1)}, u32[]{:S(2)}) copy-start(bf16[512,640]{1,0:T(8,128)(2,1)S(1)} %multiply_convert_fusion.2) | copy-start | bytes 1966084
  235.8 6.9 %copy-start.82 = (f32[512,2048]{1,0:T(8,128)S(1)}, f32[512,2048]{1,0:T(8,128)}, u32[]{:S(2)}) copy-start(f32[512,2048]{1,0:T(8,128)} %fusion.81) | copy-start | bytes 12582916
  235.8 6.9 %copy-start.87 = (f32[512,2048]{1,0:T(8,128)S(1)}, f32[512,2048]{1,0:T(8,128)}, u32[]{:S(2)}) copy-start(f32[512,2048]{1,0:T(8,128)} %get-tuple-element.351) | copy-start | bytes 12582916
  341.7 123.5 %copy-start.10 = (f32[512,256]{1,0:T(8,128)S(1)}, f32[512,256]{1,0:T(8,128)}, u32[]{:S(2)}) copy-start(f32[512,256]{1,0:T(8,128)} %copy-done.9) | copy-start | bytes 1572868
  341.7 123.5 %copy-start.59 = (f32[4,128]{1,0:T(4,128)S(1)}, f32[4,128]{1,0:T(4,128)}, u32[]{:S(2)}) copy-start(f32[4,128]{1,0:T(4,128)} %copy-done.58) | copy-start | bytes 6148
  341.7 123.5 %copy-start.72 = (f32[256]{0:T(256)S(1)}, f32[256]{0:T(256)}, u32[]{:S(2)}) copy-start(f32[256]{0:T(256)} %copy-done.71) | copy-start | bytes 3076
  341.7 123.7 %copy-start.65 = (f32[512]{0:T(512)S(1)}, f32[512]{0:T(512)}, u32[]{:S(2)}) copy-start(f32[512]{0:T(512)} %copy-done.64) | copy-start | bytes 6148
  473.5 124.8 %copy-start.61 = (f32[4,128]{1,0:T(4,128)S(1)}, f32[4,128]{1,0:T(4,128)}, u32[]{:S(2)}) copy-start(f32[4,128]{1,0:T(4,128)} %copy-done.60) | copy-start | bytes 6148
  (78 other events, 197.9 us)
Sparse Core Ops, SparseCore 0:
  9.6 21.8 all-gather.8
  36.2 49.7 all-gather.20
  88.7 47.7 all-gather.10
  138.0 16.6 all-gather.12
  156.1 25.5 all-gather.14
  183.1 25.5 all-gather.16
  210.2 25.5 all-gather.18
  314.5 149.3 reduce-scatter.1

commit v2 on v1

--- a/solution.py
+++ b/solution.py
@@ -243,6 +243,117 @@
     ] + [results[-1]]
 
 
+def gather_kernel(count, *refs):
+    shards, outs = refs[:count], refs[count : 2 * count]
+    send_sem, recv_sem, own_sem = refs[2 * count :]
+    y, z, core, x = place()
+    core_peer = device(y, z, 1 - core, x)
+    x_peer = device(y, z, core, 1 - x)
+    y_peer = device(1 - y, z, core, x)
+    greet([core_peer, x_peer, y_peer])
+
+    def send(item, slot, source, target, peer):
+        copy = pltpu.make_async_remote_copy(
+            src_ref=source,
+            dst_ref=target,
+            send_sem=send_sem.at[item, slot],
+            recv_sem=recv_sem.at[item, slot],
+            device_id=peer,
+            device_id_type=MESH_ID,
+        )
+        copy.start()
+        return copy
+
+    copies = [[None] * 5 for _ in range(count)]
+    for item in range(count):
+        copies[item][1] = send(item, 1, shards[item].at[y], outs[item].at[x, core, y], x_peer)
+    for item in range(count):
+        copies[item][0] = send(item, 0, shards[item], outs[item].at[x, core], core_peer)
+    own = [
+        pltpu.make_async_copy(shards[item], outs[item].at[x, core], own_sem.at[item])
+        for item in range(count)
+    ]
+    for copy in own:
+        copy.start()
+    for tick in range(count + 1):
+        if tick < count:
+            copies[tick][1].wait_recv()
+            here = outs[tick].at[1 - x, core, y]
+            copies[tick][2] = send(tick, 2, here, here, y_peer)
+            copies[tick][3] = send(tick, 3, here, here, core_peer)
+        if tick >= 1:
+            copies[tick - 1][2].wait_recv()
+            there = outs[tick - 1].at[1 - x, core, 1 - y]
+            copies[tick - 1][4] = send(tick - 1, 4, there, there, core_peer)
+    for item in range(count):
+        own[item].wait()
+        for slot in (0, 3, 4):
+            copies[item][slot].wait_recv()
+        for slot in range(5):
+            copies[item][slot].wait_send()
+
+
+def gather_all(shards):
+    shaped = [item.reshape(2, item.shape[0] // 2, item.shape[1]) for item in shards]
+    count = len(shards)
+    sent = sum(item.size for item in shards)
+
+    def kernel(*refs):
+        gather_kernel(count, *refs)
+
+    results = pl.pallas_call(
+        kernel,
+        out_shape=[jax.ShapeDtypeStruct((2, 2) + item.shape, item.dtype) for item in shaped],
+        in_specs=[pl.BlockSpec(memory_space=pltpu.VMEM)] * count,
+        out_specs=[pl.BlockSpec(memory_space=pltpu.VMEM)] * count,
+        scratch_shapes=[
+            pltpu.SemaphoreType.DMA((count, 5)),
+            pltpu.SemaphoreType.DMA((count, 5)),
+            pltpu.SemaphoreType.DMA((count,)),
+        ],
+        compiler_params=pltpu.CompilerParams(
+            collective_id=2, has_side_effects=True, vmem_limit_bytes=VMEM_BYTES
+        ),
+        cost_estimate=pl.CostEstimate(flops=0, bytes_accessed=10 * sent, transcendentals=0),
+        name="gather_weights",
+    )(*shaped)
+    return [
+        result.reshape(4 * item.shape[0], item.shape[1]) for result, item in zip(results, shards)
+    ]
+
+
+def gather_fast(weights, gains):
+    query, key, value, out, gate, up, down = weights
+    wide = 256
+    rows = [jnp.pad(gain, (0, wide - gain.shape[0])) for gain in gains]
+    pack = jnp.pad(jnp.stack(rows), ((0, 16 - len(rows)), (0, 0)))
+    joined, out, gate, up, down, packs = gather_all(
+        [
+            jnp.concatenate([query, key, value], axis=1),
+            out,
+            gate,
+            up,
+            down,
+            jnp.concatenate([pack, pack], axis=0),
+        ]
+    )
+    first, second = query.shape[1], query.shape[1] + key.shape[1]
+    packs = packs.reshape(4, 2, 16, wide)
+    whole_gains = [
+        packs[:, 0, at, : gain.shape[0]].reshape(4 * gain.shape[0]) for at, gain in enumerate(gains)
+    ]
+    return (
+        joined[:, :first],
+        joined[:, first:second],
+        joined[:, second:],
+        out,
+        gate,
+        up,
+        down,
+        *whole_gains,
+    )
+
+
 def gelu_mix(gate_in, up_in):
     return jax.nn.gelu(gate_in, approximate=True) * up_in
 
@@ -267,21 +378,29 @@
 ):
     seq_count, row_count, model_width = inputs.shape
     fast = lax.axis_size("ctx") == 8 and lax.axis_size("fsdp") == 4
-    gathered = (
-        lax.all_gather(query_weight, "fsdp", axis=0, tiled=True),
-        lax.all_gather(key_weight, "fsdp", axis=0, tiled=True),
-        lax.all_gather(value_weight, "fsdp", axis=0, tiled=True),
-        lax.all_gather(out_weight, "fsdp", axis=0, tiled=True),
-        lax.all_gather(gate_weight, "fsdp", axis=0, tiled=True),
-        lax.all_gather(up_weight, "fsdp", axis=0, tiled=True),
-        lax.all_gather(down_weight, "fsdp", axis=0, tiled=True),
-        lax.all_gather(pre_attn_gain, "fsdp", axis=0, tiled=True),
-        lax.all_gather(post_attn_gain, "fsdp", axis=0, tiled=True),
-        lax.all_gather(pre_ffw_gain, "fsdp", axis=0, tiled=True),
-        lax.all_gather(post_ffw_gain, "fsdp", axis=0, tiled=True),
-        lax.all_gather(query_gain, "fsdp", axis=0, tiled=True),
-        lax.all_gather(key_gain, "fsdp", axis=0, tiled=True),
-    )
+    weights = (
+        query_weight,
+        key_weight,
+        value_weight,
+        out_weight,
+        gate_weight,
+        up_weight,
+        down_weight,
+    )
+    gains = (
+        pre_attn_gain,
+        post_attn_gain,
+        pre_ffw_gain,
+        post_ffw_gain,
+        query_gain,
+        key_gain,
+    )
+    if fast:
+        gathered = gather_fast(weights, gains)
+    else:
+        gathered = tuple(
+            lax.all_gather(item, "fsdp", axis=0, tiled=True) for item in weights + gains
+        )
     (
         query_full,
         key_full,
@@ -458,13 +577,18 @@
             lax.dynamic_update_slice_in_dim(key_buffer, d_keyval, key_begin, 1),
         )
 
-    d_query_rot, key_buffer = lax.fori_loop(
-        0,
-        seq_len // key_span,
-        joint_step,
-        (query_zero, jnp.zeros((seq_count, seq_len, 2 * head_dim), jnp.float32)),
-    )
-    d_keyval_own = lax.psum_scatter(key_buffer, "ctx", scatter_dimension=1, tiled=True)
+    if seq_len <= 1024:
+        d_query_rot, key_buffer = key_grads(key_back_all, value_back_all, jnp.int32(0))
+    else:
+        d_query_rot, key_buffer = lax.fori_loop(
+            0,
+            seq_len // key_span,
+            joint_step,
+            (query_zero, jnp.zeros((seq_count, seq_len, 2 * head_dim), jnp.float32)),
+        )
+    d_keyval_own = lax.psum_scatter(
+        key_buffer.astype(jnp.bfloat16), "ctx", scatter_dimension=1, tiled=True
+    ).astype(jnp.float32)
     d_key_rot = d_keyval_own[..., :head_dim]
     d_value = d_keyval_own[..., head_dim:]
     d_query_lin, grad_query_gain = query_side_back(d_query_rot)

time: 620 us -> 472 us (0.76)
  waiting for transfers between devices: 273 us -> 140 us
  Pallas kernels: 121 us -> 171 us
  local copies, waits for them, and re-layouts: 64.7 us -> 30.7 us
  blocking collectives: 21.6 us -> 0 us
  matrix products: 81.2 us -> 69.4 us
    all_gather x5 -> x0, waiting for transfers between devices: 74.3 us -> none  [the longest x1 23.3 us: body(): lax.all_gather(gate_weight, 'fsdp', axis=0, tiled=True)]
    reduce_scatter x1, waiting for transfers between devices: 122 us -> 59.5 us  [body(): lax.psum_scatter(key_buffer.astype(jnp.bfloat16), 'ctx', scatter_dimensio...]
    pallas_call x0 -> x1, Pallas kernels: none -> 50.8 us  [gather_all(): pl.pallas_call(kernel, out_shape=[jax.ShapeDtypeStruct((2, 2) + item.shap...]
    dynamic_update_slice x4 -> x0, local copies, waits for them, and re-layouts: 19.7 us -> none  [joint_step(): lax.dynamic_update_slice_in_dim(key_buffer, d_keyval, key_begin, 1)]
    unnamed x185 -> x88, local copies, waits for them, and re-layouts: 23 us -> 8.49 us
    all_gather x2 -> x0, blocking collectives: 12.4 us -> none  [the longest x1 6.23 us: body(): lax.all_gather(value_weight, 'fsdp', axis=0, tiled=True)]
    unnamed x1 -> x0, blocking collectives: 9.19 us -> none
  transfers between devices with their start and end apart: 8 -> 3, of which waited for: 7 -> 3; matrix products, arithmetic and copies ran while one was open for 12% -> 9% of each run, Pallas kernels for 0% -> 0%
where the time goes in v2:
time: 472 us; the launch traced here: 465 us
  Pallas kernels  171 us (36%)
  waiting for transfers between devices  140 us (30%)
  matrix products  69.4 us (15%)
  other arithmetic  39.7 us (8%)
  local copies, waits for them, and re-layouts  30.7 us (7%)
  between operations  14.7 us (3%)
    pallas_call x1, Pallas kernels, reduce_all(): pl.pallas_call(kernel, out_shape=outs, in_specs=[pl.BlockSpec(memory_spac...  120 us
    reduce_scatter x1, waiting for transfers between devices, body(): lax.psum_scatter(key_buffer.astype(jnp.bfloat16), 'ctx', scatter_dimensio...  59.5 us
    pallas_call x1, Pallas kernels, gather_all(): pl.pallas_call(kernel, out_shape=[jax.ShapeDtypeStruct((2, 2) + item.shap...  50.8 us
    all_gather x1, waiting for transfers between devices, body(): value_piece = lax.all_gather(value_b, 'ctx', axis=1, tiled=True)  43.9 us
    all_gather x1, waiting for transfers between devices, body(): key_piece = lax.all_gather(key_b, 'ctx', axis=1, tiled=True)  36 us
  transfers between devices with their start and end apart: 3, of which 3 were waited for; matrix products, arithmetic and copies ran while one was open for 9% of the time, Pallas kernels for 0%

profile of v2, /device:TPU:0, one launch (start us, length us, event | category | flops | bytes accessed | tf_op | source)
XLA Modules:
  0.0 465.2 jit_solution(17191986187395042459)
XLA Ops:
  13.8 50.8 %gather_weights.1 = (bf16[2,2,2,80,1536]{4,3,2,1,0:T(8,128)(2,1)}, bf16[2,2,2,128,640]{4,3,2,1,0:T(8,128)(2,1)}, bf16[2,2,2,80,2048]{4,3,2,1,0:T(8,128)(2,1)}, b...) custom-call(bf16[2,80,1536]{2,1,0:T(8,128)(2,1)} %bitcast.252, ...), custom_call_target="tpu_custom_call" | custom-call | bytes 14008320 | tf_op jit(solution)/shard_map/gather_weights/pallas_call | solution.py:304
  76.3 2.7 multiply_reduce_fusion.3
  82.6 36.0 %all-gather.6.cloned.1.call-done = bf16[4,1024,1,256]{3,1,0,2:T(8,128)(2,1)} async-done(((bf16[4,128,1,256]{3,1,0,2:T(8,128)(2,1)}), bf16[4,1024,1,256]{3,1,0,2:T(8,128)(2,1)}) %all-gather.6.cloned.1.call-update) | async-done | bytes 2097168 | tf_op jit(solution)/shard_map/all_gather | solution.py:470
  118.7 3.3 fusion.4
  122.0 2.3 fusion.6
  125.3 43.9 %all-gather.4.cloned.1.call-done = bf16[4,1024,256]{2,1,0:T(8,128)(2,1)} async-done(((bf16[4,128,256]{2,1,0:T(8,128)(2,1)}), bf16[4,1024,256]{2,1,0:T(8,128)(2,1)}) %all-gather.4.cloned.1.call-update) | async-done | bytes 2097168 | tf_op jit(solution)/shard_map/all_gather | solution.py:471
  169.2 8.2 %fusion.32 = (bf16[4,128,4,256]{3,1,2,0:T(8,128)(2,1)S(1)}, f32[4,4,128,256]{3,2,1,0:T(8,128)}) fusion(f32[4,128,4]{1,2,0:T(4,128)S(1)} %bitcast.267, bf16[4,1024,256]{2,1,0:T(8,128)(2,1)} %all-gather.4.cloned.1.call-done, f32[4,1024,128,4]{2,1,3,0:T(8,128)} %copy-done.4, f32[4,4,128]{2,1,0:T(4,128)S(1)} %broadcast_maximum_fusion, ...), kind=kOutput, calls=%fused_computation.47 | convolution fusion | flops 1085276160 | bytes 14172160 | tf_op jit(solution)/shard_map/shqk,skd->shqd/dot_general | solution.py:477
  183.6 2.5 multiply_convert_fusion.1
  190.0 5.0 %multiply_convert_fusion = (bf16[512,2048]{1,0:T(8,128)(2,1)S(1)}, bf16[512,2048]{1,0:T(8,128)(2,1)S(1)}) fusion(f32[512,2048]{1,0:T(8,128)S(1)} %fusion.95, f32[512,2048]{1,0:T(8,128)S(1)} %get-tuple-element.93, bf16[512,640]{1,0:T(8,128)(2,1)S(1)} %get-tuple-element.66, bf16[2048,640]{1,0:T(8,128)(2,1)S(1)} %bitcast.280), kind=kOutput, calls=%fused_computation.27 | convolution fusion | flops 1367343104 | bytes 15859712 | tf_op jit(solution)/shard_map/rd,fd->rf/dot_general | solution.py:508
  197.1 2.1 multiply_reduce_fusion.4
  204.0 2.6 reshape.550
  206.6 2.9 bitcast_convert_fusion.1
  209.5 2.4 copy.57
  211.9 3.2 multiply_reduce_fusion
  215.1 5.6 %bitcast_convert_fusion = bf16[4,1024,256]{2,1,0:T(8,128)(2,1)S(1)} fusion(bf16[4,128,4,256]{1,3,2,0:T(8,128)(2,1)} %copy.57, f32[4,1024,128,4]{2,1,3,0:T(8,128)} %copy-done.4, f32[4,4,128]{2,1,0:T(4,128)S(1)} %log_add_fusion, pred[4,128,1024]{1,2,0:T(8,128)(4,1)} %broadcast_and_fusion), kind=kOutput, calls=%fused_computation.23 | convolution fusion | flops 1083179008 | bytes 12066816 | tf_op jit(solution)/shard_map/shqk,sqhd->skd/dot_general | solution.py:549
  221.2 2.8 fusion.1
  226.1 2.3 pad_maximum_fusion
  228.5 2.2 copy.59
  230.7 4.4 multiply_bitcast_fusion
  246.3 3.4 convolution_convert_fusion.2
  249.8 3.1 convolution_convert_fusion.1
  252.9 3.1 convolution_convert_fusion
  256.0 59.5 %reduce-scatter.2.cloned.1.call-done = bf16[4,128,512]{2,1,0:T(8,128)(2,1)} async-done(((bf16[4,1024,512]{2,1,0:T(8,128)(2,1)}), bf16[4,128,512]{2,1,0:T(8,128)(2,1)}) %reduce-scatter.2.cloned.1.call-update) | async-done | bytes 524304 | tf_op jit(solution)/shard_map/reduce_scatter | solution.py:589
  324.2 120.0 %reduce_grads.1 = (bf16[2,256,640]{2,1,0:T(8,128)(2,1)}, bf16[2,80,2048]{2,1,0:T(8,128)(2,1)}, bf16[2,80,2048]{2,1,0:T(8,128)(2,1)}, bf16[2,128,640]{2,1,0:T(8,1...) custom-call(bf16[2,2,2,256,640]{4,3,2,1,0:T(8,128)(2,1)} %bitcast.239, bf16[2,2,2,80,2048]{4,3,2,1,0:T(8,128)(2,1)} %bitcast.240, ...), custom_call_target="tpu_custom_call" | custom-call | flops 11141120 | bytes 22282240 | tf_op jit(solution)/shard_map/reduce_grads/pallas_call | solution.py:218
  (209 shorter events, 75.9 us)
Async XLA Ops:
  7.2 59.3 %copy-start = (bf16[4,128,640]{2,1,0:T(8,128)(2,1)S(1)}, bf16[4,128,640]{2,1,0:T(8,128)(2,1)}, u32[]{:S(2)}) copy-start(bf16[4,128,640]{2,1,0:T(8,128)(2,1)} %param.16) | copy-start | bytes 1966084
  7.2 111.5 %all-gather.6.cloned.1.call-start = ((), (), s32[]{:S(2)}) async-start(), calls=%async_computation.3 | async-start | bytes 2359296 | tf_op jit(solution)/shard_map/all_gather | solution.py:470
  69.8 99.4 %all-gather.4.cloned.1.call-start = ((), (), s32[]{:S(2)}) async-start(), calls=%async_computation.1 | async-start | bytes 2359296 | tf_op jit(solution)/shard_map/all_gather | solution.py:471
  73.0 3.2 copy-start.29
  73.0 242.5 %reduce-scatter.2.cloned.1.call-start = ((), (), s32[]{:S(2)}) async-start(), calls=%async_computation.2 | async-start | bytes 4718592 | tf_op jit(solution)/shard_map/reduce_scatter | solution.py:589
  118.7 3.4 copy-start.9
  122.0 3.2 copy-start.4
  180.4 3.2 copy-start.19
  183.6 2.5 copy-start.32
  190.0 5.0 %copy-start.17 = (bf16[512,640]{1,0:T(8,128)(2,1)}, bf16[512,640]{1,0:T(8,128)(2,1)S(1)}, u32[]{:S(2)}) copy-start(bf16[512,640]{1,0:T(8,128)(2,1)S(1)} %get-tuple-element.66) | copy-start | bytes 1966084
  211.9 8.8 %slice-start = ((s8[8388608]{0:T(1024)(128)(4,1)}), s8[4194304]{0:T(1024)(128)(4,1)S(1)}, s32[]{:S(2)}) async-start(s8[8388608]{0:T(1024)(128)(4,1)} %bitcast.234), calls=%async_computation.4 | async-start | bytes 8388608
  215.1 5.7 %slice-start.1 = ((s8[8388608]{0:T(1024)(128)(4,1)}), s8[4194304]{0:T(1024)(128)(4,1)S(1)}, s32[]{:S(2)}) async-start(s8[8388608]{0:T(1024)(128)(4,1)} %bitcast.234), calls=%async_computation.5 | async-start | bytes 8388608
  215.1 5.7 %copy-start.10 = (pred[4,128,1024]{1,2,0:T(8,128)(4,1)S(1)}, pred[4,128,1024]{1,2,0:T(8,128)(4,1)}, u32[]{:S(2)}) copy-start(pred[4,128,1024]{1,2,0:T(8,128)(4,1)} %broadcast_and_fusion) | copy-start | bytes 1572868
  215.1 5.7 %copy-start.16 = (bf16[4,128,4,256]{1,3,2,0:T(8,128)(2,1)S(1)}, bf16[4,128,4,256]{1,3,2,0:T(8,128)(2,1)}, u32[]{:S(2)}) copy-start(bf16[4,128,4,256]{1,3,2,0:T(8,128)(2,1)} %copy.57) | copy-start | bytes 3145732
  215.1 6.1 %copy-start.33 = (bf16[4,1024,256]{2,1,0:T(8,128)(2,1)S(1)}, bf16[4,1024,256]{2,1,0:T(8,128)(2,1)}, u32[]{:S(2)}) copy-start(bf16[4,1024,256]{2,1,0:T(8,128)(2,1)} %all-gather.4.cloned.1.call-done) | copy-start | bytes 6291460
  221.2 2.9 copy-start.26
  221.2 2.9 copy-start.27
  246.3 3.4 copy-start.20
  246.3 3.4 copy-start.38
  249.8 3.1 copy-start.36
  444.3 5.5 %copy-start.25 = (bf16[2,80,2048]{2,1,0:T(8,128)(2,1)S(1)}, bf16[2,80,2048]{2,1,0:T(8,128)(2,1)}, u32[]{:S(2)}) copy-start(bf16[2,80,2048]{2,1,0:T(8,128)(2,1)} %get-tuple-element.35) | copy-start | bytes 1966084
  444.3 6.8 %copy-start.24 = (bf16[2,80,2048]{2,1,0:T(8,128)(2,1)S(1)}, bf16[2,80,2048]{2,1,0:T(8,128)(2,1)}, u32[]{:S(2)}) copy-start(bf16[2,80,2048]{2,1,0:T(8,128)(2,1)} %get-tuple-element.36) | copy-start | bytes 1966084
  449.8 2.5 copy-start.23
  451.1 6.2 %copy-start.2 = (f32[512,640]{1,0:T(8,128)S(1)}, f32[512,640]{1,0:T(8,128)}, u32[]{:S(2)}) copy-start(f32[512,640]{1,0:T(8,128)} %copy-done.1) | copy-start | bytes 3932164
  (23 other events, 39.2 us)
Sparse Core Ops, SparseCore 0:
  69.9 48.7 all-gather.5
  121.4 47.7 all-gather.3
  228.6 86.9 reduce-scatter.1

commit v3 on v2

--- a/solution.py
+++ b/solution.py
@@ -467,8 +467,8 @@
 
     stat_shape = (seq_count, head_count, row_count)
     running_max = jnp.full(stat_shape, MASKED_SCORE, jnp.float32)
-    key_piece = lax.all_gather(key_b, "ctx", axis=1, tiled=True)
-    value_piece = lax.all_gather(value_b, "ctx", axis=1, tiled=True)
+    both = lax.all_gather(jnp.concatenate([key_b, value_b], axis=-1), "ctx", axis=1, tiled=True)
+    key_piece, value_piece = both[..., :head_dim], both[..., head_dim:]
     mask_now = allowed(jnp.int32(0), key_piece.shape[1])
     scores = jnp.where(mask_now, raw_scores(key_piece), MASKED_SCORE)
     new_max = jnp.maximum(running_max, jnp.max(scores, axis=-1))
@@ -554,10 +554,7 @@
         )
         return (d_query, jnp.concatenate([d_key, d_value], axis=-1))
 
-    key_back_all, value_back_all = (
-        lax.all_gather(key_b, "ctx", axis=1, tiled=True),
-        lax.all_gather(value_b, "ctx", axis=1, tiled=True),
-    )
+    key_back_all, value_back_all = key_piece, value_piece
 
     def slice_keys(key_begin, key_count):
         return (

time: 472 us -> 456 us (0.966)
  waiting for transfers between devices: 140 us -> 123 us
    all_gather x2 -> x1, waiting for transfers between devices: 80 us -> 63.4 us  [body(): lax.all_gather(jnp.concatenate([key_b, value_b], axis=-1), 'ctx', axis=1,...]
    unnamed x88 -> x90, local copies, waits for them, and re-layouts: 8.49 us -> 9.96 us
  transfers between devices with their start and end apart: 3 -> 2, of which waited for: 3 -> 2; matrix products, arithmetic and copies ran while one was open for 9% -> 8% of each run, Pallas kernels for 0% -> 0%
where the time goes in v3:
time: 456 us; the launch traced here: 449 us
  Pallas kernels  171 us (38%)
  waiting for transfers between devices  123 us (27%)
  matrix products  67.3 us (15%)
  other arithmetic  39.6 us (9%)
  local copies, waits for them, and re-layouts  32.4 us (7%)
  between operations  15.1 us (3%)
    pallas_call x1, Pallas kernels, reduce_all(): pl.pallas_call(kernel, out_shape=outs, in_specs=[pl.BlockSpec(memory_spac...  121 us
    all_gather x1, waiting for transfers between devices, body(): lax.all_gather(jnp.concatenate([key_b, value_b], axis=-1), 'ctx', axis=1,...  63.4 us
    reduce_scatter x1, waiting for transfers between devices, body(): lax.psum_scatter(key_buffer.astype(jnp.bfloat16), 'ctx', scatter_dimensio...  59.3 us
    pallas_call x1, Pallas kernels, gather_all(): pl.pallas_call(kernel, out_shape=[jax.ShapeDtypeStruct((2, 2) + item.shap...  50.8 us
    unnamed x90, local copies, waits for them, and re-layouts  9.96 us
    convert_element_type x6, other arithmetic, body(): results = [item.astype(jnp.float32) for item in results]  9.19 us
  transfers between devices with their start and end apart: 2, of which 2 were waited for; matrix products, arithmetic and copies ran while one was open for 8% of the time, Pallas kernels for 0%

profile of v3, /device:TPU:0, one launch (start us, length us, event | category | flops | bytes accessed | tf_op | source)
XLA Modules:
  0.0 448.7 jit_solution(10577603101095929483)
XLA Ops:
  13.8 50.8 %gather_weights.1 = (bf16[2,2,2,80,1536]{4,3,2,1,0:T(8,128)(2,1)}, bf16[2,2,2,128,640]{4,3,2,1,0:T(8,128)(2,1)}, bf16[2,2,2,80,2048]{4,3,2,1,0:T(8,128)(2,1)}, b...) custom-call(bf16[2,80,1536]{2,1,0:T(8,128)(2,1)} %bitcast.248, ...), custom_call_target="tpu_custom_call" | custom-call | bytes 14008320 | tf_op jit(solution)/shard_map/gather_weights/pallas_call | solution.py:304
  74.8 2.6 multiply_reduce_fusion.3
  81.0 63.4 %all-gather.2.cloned.1.call-done = bf16[4,1024,512]{2,1,0:T(8,128)(2,1)} async-done(((bf16[4,128,512]{2,1,0:T(8,128)(2,1)}), bf16[4,1024,512]{2,1,0:T(8,128)(2,1)}) %all-gather.2.cloned.1.call-update) | async-done | bytes 4194320 | tf_op jit(solution)/shard_map/all_gather | solution.py:470
  144.5 3.3 fusion.4
  150.0 2.1 copy-done.3
  153.1 4.4 fusion.26
  163.7 2.5 multiply_convert_fusion.1
  170.1 5.1 %multiply_convert_fusion = (bf16[512,2048]{1,0:T(8,128)(2,1)S(1)}, bf16[512,2048]{1,0:T(8,128)(2,1)S(1)}) fusion(f32[512,2048]{1,0:T(8,128)S(1)} %fusion.88, f32[512,2048]{1,0:T(8,128)S(1)} %get-tuple-element.93, bf16[512,640]{1,0:T(8,128)(2,1)S(1)} %get-tuple-element.66, bf16[2048,640]{1,0:T(8,128)(2,1)S(1)} %bitcast.276), kind=kOutput, calls=%fused_computation.27 | convolution fusion | flops 1367343104 | bytes 15859712 | tf_op jit(solution)/shard_map/rd,fd->rf/dot_general | solution.py:508
  177.3 2.1 multiply_reduce_fusion.4
  184.2 2.6 reshape.550
  186.8 2.8 bitcast_convert_fusion.1
  189.7 2.4 copy.57
  192.1 3.2 multiply_reduce_fusion
  195.3 5.6 %bitcast_convert_fusion = bf16[4,1024,256]{2,1,0:T(8,128)(2,1)S(1)} fusion(bf16[4,128,4,256]{1,3,2,0:T(8,128)(2,1)} %copy.57, f32[4,1024,128,4]{2,1,3,0:T(8,128)} %copy-done.3, f32[4,4,128]{2,1,0:T(4,128)S(1)} %log_add_fusion, pred[4,128,1024]{1,2,0:T(8,128)(4,1)} %broadcast_and_fusion), kind=kOutput, calls=%fused_computation.23 | convolution fusion | flops 1083179008 | bytes 12066816 | tf_op jit(solution)/shard_map/shqk,sqhd->skd/dot_general | solution.py:549
  202.0 4.1 fusion.1
  206.0 3.4 fusion.17
  209.5 2.3 pad_maximum_fusion
  211.8 2.2 copy.59
  214.0 4.4 multiply_bitcast_fusion
  229.8 3.4 convolution_convert_fusion.2
  233.2 3.1 convolution_convert_fusion.1
  236.3 3.1 convolution_convert_fusion
  239.4 59.3 %reduce-scatter.2.cloned.1.call-done = bf16[4,128,512]{2,1,0:T(8,128)(2,1)} async-done(((bf16[4,1024,512]{2,1,0:T(8,128)(2,1)}), bf16[4,128,512]{2,1,0:T(8,128)(2,1)}) %reduce-scatter.2.cloned.1.call-update) | async-done | bytes 524304 | tf_op jit(solution)/shard_map/reduce_scatter | solution.py:586
  306.8 120.7 %reduce_grads.1 = (bf16[2,256,640]{2,1,0:T(8,128)(2,1)}, bf16[2,80,2048]{2,1,0:T(8,128)(2,1)}, bf16[2,80,2048]{2,1,0:T(8,128)(2,1)}, bf16[2,128,640]{2,1,0:T(8,1...) custom-call(bf16[2,2,2,256,640]{4,3,2,1,0:T(8,128)(2,1)} %bitcast.235, bf16[2,2,2,80,2048]{4,3,2,1,0:T(8,128)(2,1)} %bitcast.236, ...), custom_call_target="tpu_custom_call" | custom-call | flops 11141120 | bytes 22282240 | tf_op jit(solution)/shard_map/reduce_grads/pallas_call | solution.py:218
  (209 shorter events, 74.7 us)
Async XLA Ops:
  7.2 59.2 %copy-start = (bf16[4,128,640]{2,1,0:T(8,128)(2,1)S(1)}, bf16[4,128,640]{2,1,0:T(8,128)(2,1)}, u32[]{:S(2)}) copy-start(bf16[4,128,640]{2,1,0:T(8,128)(2,1)} %param.16) | copy-start | bytes 1966084
  7.2 137.3 %all-gather.2.cloned.1.call-start = ((), (), s32[]{:S(2)}) async-start(), calls=%async_computation.1 | async-start | bytes 4718592 | tf_op jit(solution)/shard_map/all_gather | solution.py:470
  67.0 3.3 copy-start.5
  71.5 227.2 %reduce-scatter.2.cloned.1.call-start = ((), (), s32[]{:S(2)}) async-start(), calls=%async_computation.2 | async-start | bytes 4718592 | tf_op jit(solution)/shard_map/reduce_scatter | solution.py:586
  71.6 3.1 copy-start.29
  144.5 3.4 copy-start.8
  147.8 4.3 copy-start.3
  147.9 5.2 %copy-start.30 = (bf16[4,1024,512]{2,1,0:T(8,128)(2,1)S(1)}, bf16[4,1024,512]{2,1,0:T(8,128)(2,1)}, u32[]{:S(2)}) copy-start(bf16[4,1024,512]{2,1,0:T(8,128)(2,1)} %all-gather.2.cloned.1.call-done) | copy-start | bytes 12582916
  160.5 3.2 copy-start.19
  163.7 2.6 copy-start.34
  170.1 5.1 %copy-start.17 = (bf16[512,640]{1,0:T(8,128)(2,1)}, bf16[512,640]{1,0:T(8,128)(2,1)S(1)}, u32[]{:S(2)}) copy-start(bf16[512,640]{1,0:T(8,128)(2,1)S(1)} %get-tuple-element.66) | copy-start | bytes 1966084
  192.1 8.8 %slice-start = ((s8[8388608]{0:T(1024)(128)(4,1)}), s8[4194304]{0:T(1024)(128)(4,1)S(1)}, s32[]{:S(2)}) async-start(s8[8388608]{0:T(1024)(128)(4,1)} %bitcast.230), calls=%async_computation.3 | async-start | bytes 8388608
  195.2 5.7 %slice-start.1 = ((s8[8388608]{0:T(1024)(128)(4,1)}), s8[4194304]{0:T(1024)(128)(4,1)S(1)}, s32[]{:S(2)}) async-start(s8[8388608]{0:T(1024)(128)(4,1)} %bitcast.230), calls=%async_computation.4 | async-start | bytes 8388608
  195.2 5.7 %copy-start.9 = (pred[4,128,1024]{1,2,0:T(8,128)(4,1)S(1)}, pred[4,128,1024]{1,2,0:T(8,128)(4,1)}, u32[]{:S(2)}) copy-start(pred[4,128,1024]{1,2,0:T(8,128)(4,1)} %broadcast_and_fusion) | copy-start | bytes 1572868
  195.3 5.7 %copy-start.16 = (bf16[4,128,4,256]{1,3,2,0:T(8,128)(2,1)S(1)}, bf16[4,128,4,256]{1,3,2,0:T(8,128)(2,1)}, u32[]{:S(2)}) copy-start(bf16[4,128,4,256]{1,3,2,0:T(8,128)(2,1)} %copy.57) | copy-start | bytes 3145732
  195.3 6.7 %copy-start.31 = (bf16[4,1024,512]{2,1,0:T(8,128)(2,1)S(1)}, bf16[4,1024,512]{2,1,0:T(8,128)(2,1)}, u32[]{:S(2)}) copy-start(bf16[4,1024,512]{2,1,0:T(8,128)(2,1)} %all-gather.2.cloned.1.call-done) | copy-start | bytes 12582916
  202.0 4.1 copy-start.26
  202.0 4.1 copy-start.27
  229.8 3.4 copy-start.20
  229.8 3.4 copy-start.39
  233.2 3.1 copy-start.37
  427.5 5.5 %copy-start.25 = (bf16[2,80,2048]{2,1,0:T(8,128)(2,1)S(1)}, bf16[2,80,2048]{2,1,0:T(8,128)(2,1)}, u32[]{:S(2)}) copy-start(bf16[2,80,2048]{2,1,0:T(8,128)(2,1)} %get-tuple-element.35) | copy-start | bytes 1966084
  427.5 6.8 %copy-start.24 = (bf16[2,80,2048]{2,1,0:T(8,128)(2,1)S(1)}, bf16[2,80,2048]{2,1,0:T(8,128)(2,1)}, u32[]{:S(2)}) copy-start(bf16[2,80,2048]{2,1,0:T(8,128)(2,1)} %get-tuple-element.36) | copy-start | bytes 1966084
  434.2 6.2 %copy-start.2 = (f32[512,640]{1,0:T(8,128)S(1)}, f32[512,640]{1,0:T(8,128)}, u32[]{:S(2)}) copy-start(f32[512,640]{1,0:T(8,128)} %copy-done.1) | copy-start | bytes 3932164
  (23 other events, 40.9 us)
Sparse Core Ops, SparseCore 0:
  71.6 72.8 all-gather.1
  211.9 86.7 reduce-scatter.1
